TPU v7x, 512 devices: a whole 4x4x16 slice. The times are simulated.
512 devices in a mesh: branch: 64 (over y_hi, z, core), tensor: 8 (over y_lo, x).
Axes of the slice: x: 4, y: 4 (y_hi: 2, y_lo: 2; y = y_hi * 2 + y_lo), z: 16, core: 2. Of those that a mesh axis runs over, the one named last changes fastest.
Arguments:
- prefix_hidden: bfloat16 [4096, 8192], P('branch', 'tensor'), may hold values from -6 to 6
- key_weight: bfloat16 [8192, 1024], P('branch', 'tensor'), may hold values from -0.0625 to 0.0625
- value_weight: bfloat16 [8192, 1024], P('branch', 'tensor'), may hold values from -0.0625 to 0.0625
- suffix_q: bfloat16 [16384, 8192], P('branch', 'tensor'), may hold values from -35 to 35
- suffix_k: bfloat16 [16384, 1024], P('branch', 'tensor'), may hold values from -6 to 6
- suffix_v: bfloat16 [16384, 1024], P('branch', 'tensor'), may hold values from -6 to 6
- slab_node: int32 [64], replicated, may hold values from 0 to 11, as said below
- slab_len: int32 [64], replicated, may hold values from 1 to 64, as said below
- parent: int32 [12], replicated, may hold values from 0 to 10, as said below
- leaf: int32 [64], P('branch'), may hold values from 0 to 11
- suffix_len: int32 [64], P('branch'), may hold values from 128 to 256, as said below
Outputs:
- attended: bfloat16 [16384, 8192], P('branch', 'tensor')
Inputs may be any that keep to these rules, and one draw needn't show every extreme that they name: `slab_node`: Non-decreasing along slabs; every node holds one or more consecutive slabs. `slab_len`: every slab except the last slab of its node is full. parent[0] = 0, parent[n] < n for n >= 1, and the last node's parent is the node just before it. `suffix_len`: some group is full.
All inputs are finite; a program needn't handle non-finite values.
Results may differ from a plain program's by a relative error of at most 0.0075.
Values may be sent and summed in bfloat16 or wider, within the bound.
A program may use at most 64 MiB of HBM per device.

v0:
```python
import functools
import math

import jax
import jax.numpy as jnp
import numpy as np
from jax import lax
from jax.experimental import pallas as pl
from jax.experimental.pallas import tpu as pltpu
from jax.sharding import PartitionSpec as P

HEAD = 128
GROUP = 8
SLAB = 64
NODES = 12
SLABS = 64
NZ = 16
NX = 4
TOGETHER = 4
MESH = pl.DeviceIdType.MESH

rope_base = 500000.0
masked_score = -1e30


def place():
    branch = lax.axis_index("branch")
    tensor = lax.axis_index("tensor")
    return (
        lax.div(branch, 2 * NZ),
        lax.rem(lax.div(branch, 2), NZ),
        lax.rem(branch, 2),
        lax.div(tensor, NX),
        lax.rem(tensor, NX),
    )


def device(y_hi, z, core, y_lo, x):
    return ((y_hi * NZ + z) * 2 + core, y_lo * NX + x)


def slab_base(slab, node_ref, len_ref, parent_ref):
    node = node_ref[slab]

    def climb(unused, carried):
        current, above = carried
        upper = parent_ref[current]
        above = jnp.where(current == 0, above, above | (1 << upper))
        return upper, above

    unused, above = lax.fori_loop(0, NODES - 1, climb, (node, jnp.int32(0)))

    def count(other, total):
        other_node = node_ref[other]
        counts = ((above >> other_node) & 1) > 0
        counts = counts | ((other_node == node) & (other < slab))
        return total + jnp.where(counts, len_ref[other], 0)

    return lax.fori_loop(0, SLABS, count, jnp.int32(0))


TREE = {2: 0, 1: 0, 4: 2, 3: 2, 6: 4, 5: 4, 8: 6, 7: 6}
REACH = (NZ // 2, NZ // 2 - 1)


def children(distance, way):
    return [far for far, near in TREE.items() if near == distance and far <= REACH[way]]


def tree_kernel(
    hid,
    key_w,
    value_w,
    node_hbm,
    len_hbm,
    parent_hbm,
    leaf_ref,
    suffix_len_ref,
    freq_hbm,
    q_hbm,
    sk_hbm,
    sv_hbm,
    out_ref,
    kv,
    q_ref,
    sk_ref,
    sv_ref,
    scores,
    largest,
    top,
    mixed,
    hbuf,
    wbuf,
    sums,
    core_in,
    pair_in,
    turn,
    freq,
    node_ref,
    len_ref,
    parent_ref,
    local_sem,
    q_sem,
    a_send,
    a_recv,
    b_send,
    b_recv,
    w_send,
    w_recv,
    s_send,
    s_recv,
    g_send,
    g_recv,
    d_send,
    d_recv,
):
    y_hi, z, core, y_lo, x = place()
    sibling = device(y_hi, z, 1 - core, y_lo, x)
    partner = device(1 - y_hi, z, core, y_lo, x)
    homely = y_hi == y_lo

    def along(step):
        return device(y_hi, lax.rem(z + step + NZ, NZ), core, y_lo, x)

    def beside(step):
        return device(y_hi, z, core, y_lo, lax.rem(x + step + NX, NX))

    def remote(src, dst, send, recv, target):
        return pltpu.make_async_remote_copy(
            src_ref=src,
            dst_ref=dst,
            send_sem=send,
            recv_sem=recv,
            device_id=target,
            device_id_type=MESH,
        )

    barrier = pltpu.get_barrier_semaphore()

    def greet(target):
        pl.semaphore_signal(barrier, inc=1, device_id=target, device_id_type=MESH)

    strides = sorted({far - near for far, near in TREE.items()})
    near_by = [sibling, partner, beside(1), beside(-1)]
    for stride in strides:
        near_by += [along(stride), along(-stride)]
    for target in near_by:
        greet(target)
    for other_y in range(2):
        for other_core in range(2):
            own = homely & (other_y == y_hi) & (other_core == core)

            @pl.when(jnp.logical_not(own))
            def _():
                greet(device(other_y, z, other_core, y_hi, x))

    small = [
        pltpu.make_async_copy(src, dst, local_sem.at[number])
        for number, (src, dst) in enumerate(
            (
                (node_hbm, node_ref),
                (len_hbm, len_ref),
                (parent_hbm, parent_ref),
                (freq_hbm, freq),
                (key_w, wbuf.at[0, 0, 0]),
                (value_w, wbuf.at[0, 0, 1]),
            )
        )
    ]
    large = [
        pltpu.make_async_copy(q_hbm.at[:, pl.ds(head * HEAD, HEAD)], q_ref.at[head], q_sem.at[head])
        for head in range(GROUP)
    ]
    large.append(pltpu.make_async_copy(sk_hbm, sk_ref, q_sem.at[GROUP]))
    large.append(pltpu.make_async_copy(sv_hbm, sv_ref, q_sem.at[GROUP + 1]))
    for copy in small + large:
        copy.start()
    for copy in small:
        copy.wait()

    bases = [
        slab_base((half * NZ + z) * 2 + core, node_ref, len_ref, parent_ref) for half in range(2)
    ]
    row = lax.broadcasted_iota(jnp.int32, (2 * SLAB, HEAD), 0)
    lane = lax.broadcasted_iota(jnp.int32, (2 * SLAB, HEAD), 1)
    position = jnp.where(row < SLAB, bases[0] + row, bases[1] + row - SLAB)
    angle = position.astype(jnp.float32) * freq[...]
    turn[0] = jnp.cos(angle)
    sine = jnp.sin(angle)
    turn[1] = jnp.where(lane < HEAD // 2, -sine, sine)

    pl.semaphore_wait(barrier, 4 + len(near_by) - homely.astype(jnp.int32))

    def weight_copy(distance, way, piece):
        near = TREE[distance]
        src = wbuf.at[way if near else 0, near, piece]
        return remote(
            src,
            wbuf.at[way, distance, piece],
            w_send.at[way, distance, piece],
            w_recv.at[way, distance, piece],
            along((distance - near) * (1 - 2 * way)),
        )

    def weight_go(distance):
        for piece in range(2):
            for way in range(2):
                if distance > REACH[way]:
                    continue
                if distance:
                    weight_copy(distance, way, piece).wait_recv()
                for far in children(distance, way):
                    weight_copy(far, way, piece).start()

    weight_go(0)

    origin = core * 2 + y_hi

    def hidden_copies(other_y, other_core):
        target = device(y_lo, z, other_core, other_y, x)
        own = homely & (other_y == y_lo) & (other_core == core)
        copies = []
        for block in range(4):
            src = hid.at[:, pl.ds((2 * block + other_core) * 128, 128)]
            dst = hbuf.at[x, origin, block]
            there = a_recv.at[origin, block]
            far = remote(src, dst, a_send.at[other_y, other_core, block], there, target)
            copies.append((far, src, dst, there))
        return own, copies

    for other_y in range(2):
        for other_core in range(2):
            own, copies = hidden_copies(other_y, other_core)

            @pl.when(own)
            def _():
                for unused, src, dst, there in copies:
                    pltpu.make_async_copy(src, dst, there).start()

            @pl.when(jnp.logical_not(own))
            def _():
                for far, *unused in copies:
                    far.start()

    def beside_copy(column, source, way, hop):
        there = hbuf.at[lax.rem(column + NX, NX), source]
        return remote(
            there,
            there,
            b_send.at[hop, way, source],
            b_recv.at[hop, way, source],
            beside(1 - 2 * way),
        )

    def pass_on(source):
        for block in range(4):
            there = hbuf.at[x, source, block]
            pltpu.make_async_copy(there, there, a_recv.at[source, block]).wait()
        for way in range(2):
            beside_copy(x, source, way, 0).start()

    def beside_wait(source, way, hop):
        column = x + (hop + 1) * (2 * way - 1)
        there = hbuf.at[lax.rem(column + NX, NX), source]
        pltpu.make_async_copy(there, there, b_recv.at[hop, way, source]).wait()

    def pass_opposite(half):
        for way in range(2):
            source = way * 2 + half
            beside_wait(source, way, 0)
            beside_copy(x + 2 * way - 1, source, way, 1).start()

    def product(owner, piece):
        total = None
        for way in range(2):
            for distance in range(way, REACH[way] + 1):
                origin_z = lax.rem(z + (2 * way - 1) * distance + NZ, NZ)
                column, block = lax.div(origin_z, 4), lax.rem(origin_z, 4)
                rows = jnp.concatenate(
                    [hbuf[column, owner * 2 + half, block] for half in range(2)], axis=0
                )
                term = jnp.dot(
                    rows, wbuf[way, distance, piece], preferred_element_type=jnp.float32
                )
                total = term if total is None else total + term
        return total

    def to_core(piece):
        return remote(
            sums.at[piece, 0], core_in.at[piece], s_send.at[piece, 0], s_recv.at[piece, 0], sibling
        )

    def to_pair(piece):
        return remote(
            sums.at[piece, 1], pair_in.at[piece], s_send.at[piece, 1], s_recv.at[piece, 1], partner
        )

    def multiply(piece):
        sums[piece, 0] = product(1 - core, piece)
        to_core(piece).start()
        sums[piece, 1] = product(core, piece)

    def add_core(piece):
        to_core(piece).wait_recv()
        sums[piece, 1] = sums[piece, 1] + core_in[piece]
        to_pair(piece).start()

    def add_pair(piece):
        to_pair(piece).wait_recv()
        total = sums[piece, 1] + pair_in[piece]
        if piece == 0:
            total = total * turn[0] + pltpu.roll(total, HEAD // 2, 1) * turn[1]
        kv[core, z, piece] = total.astype(jnp.bfloat16).reshape(2, SLAB, HEAD)
        ring_go(0, piece)

    def source_z(distance, way):
        return lax.rem(z + (2 * way - 1) * distance + NZ, NZ)

    def ring_copy(distance, way, piece):
        near = TREE[distance]
        there = kv.at[core, source_z(near, way), piece]
        return remote(
            there,
            there,
            g_send.at[way, distance, piece],
            g_recv.at[way, distance, piece],
            along((distance - near) * (1 - 2 * way)),
        )

    def across_copy(distance, way, piece):
        there = kv.at[core, source_z(distance, way), piece]
        return remote(
            there,
            there,
            d_send.at[way, distance, piece],
            d_recv.at[way, distance, piece],
            sibling,
        )

    def ring_go(distance, piece):
        for way in range(2):
            if distance > REACH[way]:
                continue
            if distance:
                there = kv.at[core, source_z(distance, way), piece]
                pltpu.make_async_copy(there, there, g_recv.at[way, distance, piece]).wait()
            for far in children(distance, way):
                ring_copy(far, way, piece).start()

    def across_go(distance, piece):
        for way in range(2):
            if way <= distance <= REACH[way]:
                across_copy(distance, way, piece).start()

    factor = math.log2(math.e) / math.sqrt(HEAD)
    rows = q_ref.shape[1]

    def climb(unused, carried):
        current, path = carried
        return parent_ref[current], path | (1 << current)

    unused, path = lax.fori_loop(0, NODES, climb, (leaf_ref[0], jnp.int32(0)))

    def heads(body):
        def some(step, unused):
            for number in range(TOGETHER):
                body(step * TOGETHER + number)
            return 0

        lax.fori_loop(0, GROUP // TOGETHER, some, 0)

    def against(head, key_block):
        return lax.dot_general(
            q_ref[head], key_block, (((1,), (1,)), ((), ())), preferred_element_type=jnp.float32
        )

    def fold(score):
        most = score[:, :HEAD]
        for start in range(HEAD, score.shape[1], HEAD):
            most = jnp.maximum(most, score[:, start : start + HEAD])
        return most

    def weigh(score, most, value_block):
        wide = jnp.concatenate([most] * (score.shape[1] // HEAD), axis=1)
        weights = jnp.exp2(score * factor - wide).astype(jnp.bfloat16)
        wider = jnp.concatenate([value_block, jnp.ones_like(value_block)], axis=1)
        return jnp.dot(weights, wider, preferred_element_type=jnp.float32)

    def block_of(owner, places, piece):
        return jnp.concatenate(
            [kv[owner, source_z(d, way), piece].reshape(2 * SLAB, HEAD) for way, d in places], axis=0
        )

    def score_block(number, owner, places):
        width = len(places) * 2 * SLAB
        position = lax.broadcasted_iota(jnp.int32, (1, width), 1)
        limit = jnp.zeros((1, width), jnp.int32)
        for place_number, (way, d) in enumerate(places):
            for half in range(2):
                slab = (half * NZ + source_z(d, way)) * 2 + owner
                live = ((path >> node_ref[slab]) & 1) * len_ref[slab]
                start = (2 * place_number + half) * SLAB
                limit = jnp.where(position >= start, start + live, limit)
        bias = jnp.where(position < limit, 0.0, masked_score)
        key_block = block_of(owner, places, 0)

        def body(head):
            score = against(head, key_block) + bias
            scores[number, head, :, :width] = score
            most = fold(score)
            largest[head] = jnp.maximum(largest[head], most) if number else most

        heads(body)

    def raise_top():
        def body(head):
            most = jnp.max(largest[head], axis=1, keepdims=True) * factor
            before = top[head]
            after = jnp.maximum(before, most)
            top[head] = after
            shrink = jnp.exp2(before - after)
            mixed[head] = mixed[head] * jnp.concatenate([shrink, shrink], axis=1)

        heads(body)

    def weigh_block(number, owner, places):
        width = len(places) * 2 * SLAB
        value_block = block_of(owner, places, 1)

        def body(head):
            mixed[head] += weigh(scores[number, head, :, :width], top[head], value_block)

        heads(body)

    def attend_suffix():
        for copy in large:
            copy.wait()
        query_pos = lax.broadcasted_iota(jnp.int32, (rows, rows), 0)
        key_pos = lax.broadcasted_iota(jnp.int32, (rows, rows), 1)
        mask = (key_pos <= query_pos) & (key_pos < suffix_len_ref[0])
        key_block, value_block = sk_ref[...], sv_ref[...]

        def body(head):
            score = jnp.where(mask, against(head, key_block), masked_score)
            most = jnp.max(score, axis=1, keepdims=True) * factor
            top[head] = jnp.broadcast_to(most, (rows, HEAD))
            mixed[head] = weigh(score, top[head], value_block)

        heads(body)

    def across_wait(places):
        for way, d in places:
            for piece in range(2):
                there = kv.at[1 - core, source_z(d, way), piece]
                pltpu.make_async_copy(there, there, d_recv.at[way, d, piece]).wait()

    def attend_places(places):
        score_block(0, core, places)
        across_wait(places)
        score_block(1, 1 - core, places)
        raise_top()
        weigh_block(0, core, places)
        weigh_block(1, 1 - core, places)

    first, second = y_lo, 1 - y_lo
    weight_go(2)
    pass_on(first)
    pass_on(2 + first)
    weight_go(1)
    weight_go(4)
    pass_on(second)
    pass_on(2 + second)
    weight_go(3)
    pass_opposite(first)
    attend_suffix()
    weight_go(6)
    weight_go(5)
    pass_opposite(second)
    for half in (first, second):
        for way in range(2):
            beside_wait((1 - way) * 2 + half, way, 0)
    weight_go(8)
    weight_go(7)
    for half in (first, second):
        for way in range(2):
            beside_wait(way * 2 + half, way, 1)
    multiply(0)
    multiply(1)
    add_core(0)
    add_core(1)
    add_pair(0)
    add_pair(1)
    across_go(0, 0)
    across_go(0, 1)
    attend_places(((0, 0),))
    for stage in range(1, 5):
        for distance in (2 * stage, 2 * stage - 1):
            for piece in range(2):
                ring_go(distance, piece)
            for piece in range(2):
                across_go(distance, piece)
        attend_places(
            [
                (way, distance)
                for way in range(2)
                for distance in (2 * stage - 1, 2 * stage)
                if distance <= REACH[way]
            ]
        )
    for head in range(GROUP):
        result = mixed[head, :, :HEAD] / mixed[head, :, HEAD:]
        out_ref[:, head * HEAD : (head + 1) * HEAD] = result.astype(jnp.bfloat16)

    for way in range(2):
        for distance in range(way, REACH[way] + 1):
            for piece in range(2):
                across_copy(distance, way, piece).wait_send()
                if distance:
                    ring_copy(distance, way, piece).wait_send()
                    weight_copy(distance, way, piece).wait_send()
        for source in range(4):
            beside_copy(x, source, way, 0).wait_send()
        for half in range(2):
            beside_copy(x, way * 2 + half, way, 1).wait_send()
    for other_y in range(2):
        for other_core in range(2):
            own, copies = hidden_copies(other_y, other_core)

            @pl.when(jnp.logical_not(own))
            def _():
                for far, *unused in copies:
                    far.wait_send()

    for piece in range(2):
        to_core(piece).wait_send()
        to_pair(piece).wait_send()


def attend(hid, key_w, value_w, q, sk, sv, slab_node, slab_len, parent, leaf, suffix_len):
    freqs = rope_base ** (-2.0 * np.arange(HEAD // 2, dtype=np.float64) / HEAD)
    freqs = jnp.asarray(np.tile(freqs, 2)[None, :].astype(np.float32))
    dma = pltpu.SemaphoreType.DMA
    hbm = pl.BlockSpec(memory_space=pltpu.HBM)
    vmem = pl.BlockSpec(memory_space=pltpu.VMEM)
    rows = q.shape[0]
    smem = pl.BlockSpec(memory_space=pltpu.SMEM)

    def stay(*arrays):
        return [pltpu.with_memory_space_constraint(array, pltpu.HBM) for array in arrays]

    operands = [
        *stay(hid, key_w, value_w, slab_node, slab_len, parent),
        leaf,
        suffix_len,
        *stay(freqs, q, sk, sv),
    ]
    return pl.pallas_call(
        tree_kernel,
        out_shape=jax.ShapeDtypeStruct(q.shape, jnp.bfloat16),
        in_specs=[hbm] * 6 + [smem] * 2 + [hbm] * 4,
        out_specs=vmem,
        scratch_shapes=[
            pltpu.VMEM((2, NZ, 2, 2, SLAB, HEAD), jnp.bfloat16),
            pltpu.VMEM((GROUP, rows, HEAD), jnp.bfloat16),
            pltpu.VMEM((rows, HEAD), jnp.bfloat16),
            pltpu.VMEM((rows, HEAD), jnp.bfloat16),
            pltpu.VMEM((2, GROUP, rows, 8 * SLAB), jnp.float32),
            pltpu.VMEM((GROUP, rows, HEAD), jnp.float32),
            pltpu.VMEM((GROUP, rows, HEAD), jnp.float32),
            pltpu.VMEM((GROUP, rows, 2 * HEAD), jnp.float32),
            pltpu.VMEM((NX, 4, 4, SLAB, 128), jnp.bfloat16),
            pltpu.VMEM((2, 9, 2, 128, 128), jnp.bfloat16),
            pltpu.VMEM((2, 2, 2 * SLAB, HEAD), jnp.float32),
            pltpu.VMEM((2, 2 * SLAB, HEAD), jnp.float32),
            pltpu.VMEM((2, 2 * SLAB, HEAD), jnp.float32),
            pltpu.VMEM((2, 2 * SLAB, HEAD), jnp.float32),
            pltpu.VMEM((1, HEAD), jnp.float32),
            pltpu.SMEM((SLABS,), jnp.int32),
            pltpu.SMEM((SLABS,), jnp.int32),
            pltpu.SMEM((NODES,), jnp.int32),
            dma((6,)),
            dma((GROUP + 2,)),
            dma((2, 2, 4)),
            dma((4, 4)),
            dma((2, 2, 4)),
            dma((2, 2, 4)),
            dma((2, 9, 2)),
            dma((2, 9, 2)),
            dma((2, 2)),
            dma((2, 2)),
            dma((2, 9, 2)),
            dma((2, 9, 2)),
            dma((2, 9, 2)),
            dma((2, 9, 2)),
        ],
        compiler_params=pltpu.CompilerParams(
            collective_id=0, has_side_effects=True, vmem_limit_bytes=48 << 20
        ),
        cost_estimate=pl.CostEstimate(
            flops=5_000_000_000, bytes_accessed=4_000_000, transcendentals=9_000_000
        ),
        name="attend_tree",
    )(*operands)


def local(
    prefix_hidden,
    key_weight,
    value_weight,
    suffix_q,
    suffix_k,
    suffix_v,
    slab_node,
    slab_len,
    parent,
    leaf,
    suffix_len,
):
    return attend(
        prefix_hidden,
        key_weight,
        value_weight,
        suffix_q,
        suffix_k,
        suffix_v,
        slab_node,
        slab_len,
        parent,
        leaf,
        suffix_len,
    )


def solution(mesh):
    return jax.shard_map(
        local,
        mesh=mesh,
        in_specs=(
            P("branch", "tensor"),
            P("branch", "tensor"),
            P("branch", "tensor"),
            P("branch", "tensor"),
            P("branch", "tensor"),
            P("branch", "tensor"),
            P(),
            P(),
            P(),
            P("branch"),
            P("branch"),
        ),
        out_specs=P("branch", "tensor"),
        check_vma=False,
    )
```

profile of v0, /device:TPU:1, one launch (start us, length us, event | category | flops | bytes accessed | tf_op | source)
XLA Modules:
  0.0 73.4 jit_solution(13987112801994578866)
XLA Ops:
  1.3 71.3 %attend_tree.1 = bf16[256,1024]{1,0:T(8,128)(2,1)S(1)} custom-call(bf16[64,1024]{1,0:T(8,128)(2,1)} %hid.1, bf16[128,128]{1,0:T(8,128)(2,1)} %key_w.1, bf16[128,128]{1,0:T(8,128)(2,1)} %value_w.1, s32[64]{0:T(128)} %node_hbm.1, s32[64]{0:T(128)} %len_hbm.1, s32[12]{0:T(128)} %parent_hbm.1, s32[1]{0:T(128)S(6)} %copy.14.leaf_ref, s32[1]{0:T(128)S(6)} %copy.15.suffix_len_ref, ...), custom_call_target="tpu_custom_call" | custom-call | flops 5000000000 | bytes 4000000 | tf_op jit(solution)/shard_map/attend_tree/pallas_call | solution.py:557
  72.6 0.8 %copy.16 = bf16[256,1024]{1,0:T(8,128)(2,1)} copy(bf16[256,1024]{1,0:T(8,128)(2,1)S(1)} %attend_tree.1) | data formatting | bytes 1048576
where the time goes:
time: 73.6 us; the launch traced here: 73.4 us
  Pallas kernels  71.3 us (97%)
  between operations  1.3 us (2%)
  local copies, waits for them, and re-layouts  0.8 us (1%)
    pallas_call x1, Pallas kernels, attend(): pl.pallas_call(tree_kernel, out_shape=jax.ShapeDtypeStruct(q.shape, jnp.b...  71.3 us

commit v1 on v0

--- a/solution.py
+++ b/solution.py
@@ -16,7 +16,7 @@
 SLABS = 64
 NZ = 16
 NX = 4
-TOGETHER = 4
+TOGETHER = 8
 MESH = pl.DeviceIdType.MESH
 
 rope_base = 500000.0

time: 73.6 us -> 71.3 us (0.969)
  Pallas kernels: 71.3 us -> 69 us
    pallas_call x1, Pallas kernels: 71.3 us -> 69 us  [attend(): pl.pallas_call(tree_kernel, out_shape=jax.ShapeDtypeStruct(q.shape, jnp.b...]
where the time goes in v1:
time: 71.3 us; the launch traced here: 71.1 us
  Pallas kernels  69 us (97%)
  between operations  1.31 us (2%)
  local copies, waits for them, and re-layouts  0.8 us (1%)
    pallas_call x1, Pallas kernels, attend(): pl.pallas_call(tree_kernel, out_shape=jax.ShapeDtypeStruct(q.shape, jnp.b...  69 us

profile of v1, /device:TPU:1, one launch (start us, length us, event | category | flops | bytes accessed | tf_op | source)
XLA Modules:
  0.0 71.1 jit_solution(14148871295040519005)
XLA Ops:
  1.3 69.0 %attend_tree.1 = bf16[256,1024]{1,0:T(8,128)(2,1)S(1)} custom-call(bf16[64,1024]{1,0:T(8,128)(2,1)} %hid.1, bf16[128,128]{1,0:T(8,128)(2,1)} %key_w.1, bf16[128,128]{1,0:T(8,128)(2,1)} %value_w.1, s32[64]{0:T(128)} %node_hbm.1, s32[64]{0:T(128)} %len_hbm.1, s32[12]{0:T(128)} %parent_hbm.1, s32[1]{0:T(128)S(6)} %copy.14.leaf_ref, s32[1]{0:T(128)S(6)} %copy.15.suffix_len_ref, ...), custom_call_target="tpu_custom_call" | custom-call | flops 5000000000 | bytes 4000000 | tf_op jit(solution)/shard_map/attend_tree/pallas_call | solution.py:557
  70.3 0.8 %copy.16 = bf16[256,1024]{1,0:T(8,128)(2,1)} copy(bf16[256,1024]{1,0:T(8,128)(2,1)S(1)} %attend_tree.1) | data formatting | bytes 1048576

commit v2 on v1

--- a/solution.py
+++ b/solution.py
@@ -295,11 +295,6 @@
             sums.at[piece, 1], pair_in.at[piece], s_send.at[piece, 1], s_recv.at[piece, 1], partner
         )
 
-    def multiply(piece):
-        sums[piece, 0] = product(1 - core, piece)
-        to_core(piece).start()
-        sums[piece, 1] = product(core, piece)
-
     def add_core(piece):
         to_core(piece).wait_recv()
         sums[piece, 1] = sums[piece, 1] + core_in[piece]
@@ -484,8 +479,11 @@
     for half in (first, second):
         for way in range(2):
             beside_wait(way * 2 + half, way, 1)
-    multiply(0)
-    multiply(1)
+    for piece in range(2):
+        sums[piece, 0] = product(1 - core, piece)
+        to_core(piece).start()
+    for piece in range(2):
+        sums[piece, 1] = product(core, piece)
     add_core(0)
     add_core(1)
     add_pair(0)

time: 71.3 us -> 71.3 us (level)
  no operation moved by 1% of the time
where the time goes in v2:
time: 71.3 us; the launch traced here: 71.1 us
  Pallas kernels  69 us (97%)
  between operations  1.31 us (2%)
  local copies, waits for them, and re-layouts  0.8 us (1%)
    pallas_call x1, Pallas kernels, attend(): pl.pallas_call(tree_kernel, out_shape=jax.ShapeDtypeStruct(q.shape, jnp.b...  69 us

profile of v2, /device:TPU:1, one launch (start us, length us, event | category | flops | bytes accessed | tf_op | source)
XLA Modules:
  0.0 71.1 jit_solution(4111522951056434032)
XLA Ops:
  1.3 69.0 %attend_tree.1 = bf16[256,1024]{1,0:T(8,128)(2,1)S(1)} custom-call(bf16[64,1024]{1,0:T(8,128)(2,1)} %hid.1, bf16[128,128]{1,0:T(8,128)(2,1)} %key_w.1, bf16[128,128]{1,0:T(8,128)(2,1)} %value_w.1, s32[64]{0:T(128)} %node_hbm.1, s32[64]{0:T(128)} %len_hbm.1, s32[12]{0:T(128)} %parent_hbm.1, s32[1]{0:T(128)S(6)} %copy.14.leaf_ref, s32[1]{0:T(128)S(6)} %copy.15.suffix_len_ref, ...), custom_call_target="tpu_custom_call" | custom-call | flops 5000000000 | bytes 4000000 | tf_op jit(solution)/shard_map/attend_tree/pallas_call | solution.py:555
  70.3 0.8 %copy.16 = bf16[256,1024]{1,0:T(8,128)(2,1)} copy(bf16[256,1024]{1,0:T(8,128)(2,1)S(1)} %attend_tree.1) | data formatting | bytes 1048576
